TPU v7x, 32 devices: a whole 2x2x4 slice. The times are simulated.
32 devices in a mesh: fr: 4 (over x, core), fc: 8 (over z, y).
Axes of the slice: x: 2, y: 2, z: 4, core: 2. Of those that a mesh axis runs over, the one named last changes fastest.
Arguments:
- front_slab: float32 [2048, 24576], P('fr', 'fc'), may hold values from -6 to 6
- panels: float32 [4, 24576, 256], P(None, 'fc'), may hold values from -8 to 8
- diagonal_blocks: float32 [4, 256, 256], P(None, None, 'fc'), may hold values from -3 to 96, as said below
- extend_maps: int32 [4, 4, 8, 128], P(None, 'fr', 'fc'), may hold values from 0 to 127, each once within a row
Outputs:
- front_out: float32 [2048, 24576], P('fr', 'fc')
Inputs may be any that keep to these rules, and one draw needn't show every extreme that they name: `extend_maps`: each level's map at each grid position names every row of the block once. `diagonal_blocks`: the symmetric part of each block is positive definite.
All inputs are finite; a program needn't handle non-finite values.
Results may differ from a plain program's by a relative error of at most 0.0001.
Values sent between devices are 32-bit elements; how exact they have to be, the bound alone decides.
A program may use at most 128 MiB of HBM per device.

v0:
```python
import jax
import jax.numpy as jnp
from jax import lax
from jax.sharding import PartitionSpec as P

HIGHEST = lax.Precision.HIGHEST


def partner(x, axis, distance):
    return lax.ppermute(x, axis, [(i, i ^ 1 << distance) for i in range(lax.axis_size(axis))])


def broadcast(block, axis, source):
    block = jnp.where(lax.axis_index(axis) == source, block, jnp.zeros_like(block))
    return lax.psum(block, axis)


def inverse_factor(diagonal_block):
    symmetric = 0.5 * (diagonal_block + diagonal_block.T)
    lower_factor = jnp.linalg.cholesky(symmetric)
    identity = jnp.eye(symmetric.shape[0], dtype=symmetric.dtype)
    return lax.linalg.triangular_solve(lower_factor, identity, left_side=True, lower=True)


def swap_columns(top_rows, bit_index):
    return partner(top_rows, "fc", bit_index)


def swap_rows(top_rows, bit_index):
    return partner(top_rows, "fr", bit_index)


def merge_top(front_slab, received, row_map):
    block_rows = row_map.shape[0]
    moved_rows = jnp.take(received, row_map, axis=0)
    return lax.dynamic_update_slice(front_slab, front_slab[:block_rows] + moved_rows, (0, 0))


def body(front_slab, panels, diagonal_blocks, extend_maps):
    row_count, col_count = front_slab.shape
    block_rows = extend_maps.shape[3]
    row_index = lax.axis_index("fr")
    row_devices = lax.axis_size("fr")
    col_devices = lax.axis_size("fc")
    whole_diagonal = lax.all_gather(diagonal_blocks, "fc", axis=2, tiled=True)
    partner_plan = [
        (True, col_devices.bit_length() - 2),
        (True, 0),
        (False, row_devices.bit_length() - 2),
        (False, 0),
    ]
    pending = None
    for level_index in range(4):
        use_columns, bit_index = partner_plan[level_index]
        top_rows = front_slab[:block_rows]
        received = (
            swap_columns(top_rows, bit_index) if use_columns else swap_rows(top_rows, bit_index)
        )
        front_slab = merge_top(front_slab, received, extend_maps[level_index, 0, 0])
        inverse = inverse_factor(whole_diagonal[level_index])
        panel_level = panels[level_index]
        column_factor = jnp.dot(panel_level, inverse.T, precision=HIGHEST)
        first_row = row_index * row_count
        source = lax.dynamic_slice_in_dim(column_factor, first_row % col_count, row_count, 0)
        slab_factor = broadcast(source, "fc", first_row // col_count)
        front_slab = front_slab - jnp.dot(slab_factor, column_factor.T, precision=HIGHEST)
    return front_slab


def solution(mesh):
    in_specs = (P("fr", "fc"), P(None, "fc", None), P(None, None, "fc"), P(None, "fr", "fc", None))
    out_specs = P("fr", "fc")
    return jax.shard_map(body, mesh=mesh, in_specs=in_specs, out_specs=out_specs, check_vma=False)
```

profile of v0, /device:TPU:25, one launch (start us, length us, event | category | flops | bytes accessed | tf_op | source)
XLA Modules:
  0.0 627.0 jit_solution(12572764727517571125)
XLA Ops:
  16.5 94.0 %all-gather.2.cloned.1.call-done = f32[4,256,256]{1,0,2:T(4,128)} async-done(((f32[4,256,32]{1,0,2:T(4,128)}), f32[4,256,256]{1,0,2:T(4,128)}) %all-gather.2.cloned.1.call-update) | async-done | bytes 1048592 | tf_op jit(solution)/shard_map/all_gather | solution.py:45
  117.1 11.7 %cholesky.214 = f32[128,128]{1,0:T(8,128)S(1)} custom-call(f32[128,128]{1,0:T(8,128)S(1)} %cholesky.346), custom_call_target="Cholesky" | custom-call | tf_op jit(solution)/shard_map/jit(cholesky)/cholesky | solution.py:20
  128.8 9.8 %custom-call.17 = f32[1,128,128]{1,2,0:T(8,128)S(1)} custom-call(f32[1,128,128]{2,1,0:T(8,128)S(1)} %get-tuple-element.109), custom_call_target="InvertDiagBlocksLowerTriangular" | custom-call | tf_op jit(solution)/shard_map/jit(cholesky)/cholesky | solution.py:20
  139.1 11.7 %cholesky.231 = f32[128,128]{1,0:T(8,128)S(1)} custom-call(f32[128,128]{1,0:T(8,128)S(1)} %convolution_subtract_fusion.11), custom_call_target="Cholesky" | custom-call | tf_op jit(solution)/shard_map/jit(cholesky)/cholesky | solution.py:20
  157.6 20.0 %custom-call.18 = f32[2,128,128]{1,2,0:T(8,128)S(1)} custom-call(f32[2,128,128]{2,1,0:T(8,128)S(1)} %get-tuple-element.34), custom_call_target="InvertDiagBlocksLowerTriangular" | custom-call | tf_op jit(solution)/shard_map/triangular_solve/custom-call.0 | solution.py:22
  178.7 11.7 %cholesky.248 = f32[128,128]{1,0:T(8,128)S(1)} custom-call(f32[128,128]{1,0:T(8,128)S(1)} %cholesky.349), custom_call_target="Cholesky" | custom-call | tf_op jit(solution)/shard_map/jit(cholesky)/cholesky | solution.py:20
  190.5 9.8 %custom-call.19 = f32[1,128,128]{1,2,0:T(8,128)S(1)} custom-call(f32[1,128,128]{2,1,0:T(8,128)S(1)} %get-tuple-element.105), custom_call_target="InvertDiagBlocksLowerTriangular" | custom-call | tf_op jit(solution)/shard_map/jit(cholesky)/cholesky | solution.py:20
  200.8 11.7 %cholesky.265 = f32[128,128]{1,0:T(8,128)S(1)} custom-call(f32[128,128]{1,0:T(8,128)S(1)} %convolution_subtract_fusion.10), custom_call_target="Cholesky" | custom-call | tf_op jit(solution)/shard_map/jit(cholesky)/cholesky | solution.py:20
  219.5 19.8 %custom-call.20 = f32[2,128,128]{1,2,0:T(8,128)S(1)} custom-call(f32[2,128,128]{2,1,0:T(8,128)S(1)} %get-tuple-element.35), custom_call_target="InvertDiagBlocksLowerTriangular" | custom-call | tf_op jit(solution)/shard_map/triangular_solve/custom-call.0 | solution.py:22
  253.5 11.7 %cholesky.282 = f32[128,128]{1,0:T(8,128)S(1)} custom-call(f32[128,128]{1,0:T(8,128)S(1)} %cholesky.352), custom_call_target="Cholesky" | custom-call | tf_op jit(solution)/shard_map/jit(cholesky)/cholesky | solution.py:20
  265.3 10.0 %custom-call.21 = f32[1,128,128]{1,2,0:T(8,128)S(1)} custom-call(f32[1,128,128]{2,1,0:T(8,128)S(1)} %get-tuple-element.101), custom_call_target="InvertDiagBlocksLowerTriangular" | custom-call | tf_op jit(solution)/shard_map/jit(cholesky)/cholesky | solution.py:20
  275.8 11.7 %cholesky.299 = f32[128,128]{1,0:T(8,128)S(1)} custom-call(f32[128,128]{1,0:T(8,128)S(1)} %convolution_subtract_fusion.9), custom_call_target="Cholesky" | custom-call | tf_op jit(solution)/shard_map/jit(cholesky)/cholesky | solution.py:20
  294.5 20.1 %custom-call.22 = f32[2,128,128]{1,2,0:T(8,128)S(1)} custom-call(f32[2,128,128]{2,1,0:T(8,128)S(1)} %get-tuple-element.36), custom_call_target="InvertDiagBlocksLowerTriangular" | custom-call | tf_op jit(solution)/shard_map/triangular_solve/custom-call.0 | solution.py:22
  322.0 11.7 %cholesky.316 = f32[128,128]{1,0:T(8,128)S(1)} custom-call(f32[128,128]{1,0:T(8,128)S(1)} %cholesky.355), custom_call_target="Cholesky" | custom-call | tf_op jit(solution)/shard_map/jit(cholesky)/cholesky | solution.py:20
  333.8 9.8 %custom-call.23 = f32[1,128,128]{1,2,0:T(8,128)S(1)} custom-call(f32[1,128,128]{2,1,0:T(8,128)S(1)} %get-tuple-element.97), custom_call_target="InvertDiagBlocksLowerTriangular" | custom-call | tf_op jit(solution)/shard_map/jit(cholesky)/cholesky | solution.py:20
  344.1 11.9 %cholesky.333 = f32[128,128]{1,0:T(8,128)S(1)} custom-call(f32[128,128]{1,0:T(8,128)S(1)} %convolution_subtract_fusion.8), custom_call_target="Cholesky" | custom-call | tf_op jit(solution)/shard_map/jit(cholesky)/cholesky | solution.py:20
  363.0 19.7 %custom-call.24 = f32[2,128,128]{1,2,0:T(8,128)S(1)} custom-call(f32[2,128,128]{2,1,0:T(8,128)S(1)} %get-tuple-element.37), custom_call_target="InvertDiagBlocksLowerTriangular" | custom-call | tf_op jit(solution)/shard_map/triangular_solve/custom-call.0 | solution.py:22
  400.3 99.6 %all-reduce.4.cloned.1.call-done = (f32[512,256]{0,1:T(8,128)}, f32[512,256]{0,1:T(8,128)}, f32[512,256]{0,1:T(8,128)}, f32[512,256]{0,1:T(8,128)}) async-done(((f32[512,256]{0,1:T(8,128)}, f32[512,256]{0,1:T(8,128)}, f32[512,256]{0,1:T(8,128)}, f32[512,256]{0,1:T(8,128)}), (f32[512,256]{0,1:T(8,128)}, f32[512,256]{0,1:T(8,128)}, f32[512,256]{0,1:T(8,128)}, ...) | async-done | bytes 2097168 | tf_op jit(solution)/shard_map/psum | solution.py:15
  499.9 8.1 %convolution_subtract_fusion.3 = f32[512,3072]{1,0:T(8,128)S(1)} fusion(f32[512,3072]{1,0:T(8,128)} %fusion.15, f32[512,256]{0,1:T(8,128)} %get-tuple-element.70, f32[256,3072]{1,0:T(8,128)} %fusion.6), kind=kOutput, calls=%fused_computation.15 | convolution fusion | flops 4833411072 | bytes 16252928 | tf_op jit(solution)/shard_map/dot_general | solution.py:66
  510.7 32.7 %collective-permute-done.1 = f32[128,3072]{1,0:T(8,128)S(1)} collective-permute-done((f32[128,3072]{1,0:T(8,128)S(1)}, f32[128,3072]{1,0:T(8,128)S(1)}, u32[]{:S(2)}, u32[]{:S(2)}) %collective-permute-start.1) | collective-permute-done | bytes 1572896 | tf_op jit(solution)/shard_map/ppermute | solution.py:10
  547.5 7.3 %convolution_subtract_fusion.2 = f32[512,3072]{1,0:T(8,128)S(1)} fusion(f32[512,3072]{1,0:T(8,128)} %fusion.14, f32[512,256]{0,1:T(8,128)S(1)} %copy-done.9, f32[256,3072]{1,0:T(8,128)S(1)} %copy-done.3), kind=kOutput, calls=%fused_computation.14 | convolution fusion | flops 4833411072 | bytes 16252928 | tf_op jit(solution)/shard_map/dot_general | solution.py:66
  557.5 32.2 %collective-permute-done.2 = f32[128,3072]{1,0:T(8,128)S(1)} collective-permute-done((f32[128,3072]{1,0:T(8,128)S(1)}, f32[128,3072]{1,0:T(8,128)S(1)}, u32[]{:S(2)}, u32[]{:S(2)}) %collective-permute-start.2) | collective-permute-done | bytes 1572896 | tf_op jit(solution)/shard_map/ppermute | solution.py:10
  593.9 7.3 %convolution_subtract_fusion.1 = f32[512,3072]{1,0:T(8,128)S(1)} fusion(f32[512,3072]{1,0:T(8,128)} %fusion.13, f32[512,256]{0,1:T(8,128)S(1)} %copy-done.8, f32[256,3072]{1,0:T(8,128)S(1)} %copy-done.4), kind=kOutput, calls=%fused_computation.13 | convolution fusion | flops 4833411072 | bytes 16252928 | tf_op jit(solution)/shard_map/dot_general | solution.py:66
  610.8 9.0 %convolution_subtract_fusion = f32[512,3072]{1,0:T(8,128)} fusion(f32[512,3072]{1,0:T(8,128)} %fusion.12, f32[512,256]{0,1:T(8,128)S(1)} %copy-done.7, f32[256,3072]{1,0:T(8,128)S(1)} %copy-done.6), kind=kOutput, calls=%fused_computation.12 | convolution fusion | flops 4833411072 | bytes 16252928 | tf_op jit(solution)/shard_map/dot_general | solution.py:66
  (159 shorter events, 120.7 us)
Async XLA Ops:
  6.5 6.3 %copy-start.10 = (f32[4,256,32]{1,2,0:T(8,128)S(1)}, f32[4,256,32]{1,2,0:T(8,128)}, u32[]{:S(2)}) copy-start(f32[4,256,32]{1,2,0:T(8,128)} %param.11) | copy-start | bytes 393220
  6.5 103.9 %all-gather.2.cloned.1.call-start = ((), (), s32[]{:S(2)}) async-start(), calls=%async_computation | async-start | bytes 1179648 | tf_op jit(solution)/shard_map/all_gather | solution.py:45
  13.6 486.3 %all-reduce.4.cloned.1.call-start = ((), (), s32[]{:S(2)}) async-start(), calls=%async_computation.1 | async-start | bytes 4194304 | tf_op jit(solution)/shard_map/psum | solution.py:15
  16.4 379.9 %collective-permute-start = (f32[128,3072]{1,0:T(8,128)}, f32[128,3072]{1,0:T(8,128)S(1)}, u32[]{:S(2)}, u32[]{:S(2)}) collective-permute-start(f32[128,3072]{1,0:T(8,128)} %slice.90), channel_id=1, source_target_pairs={{0,4},{1,5},{2,6},{3,7},{4,0},{5,1},{6,2},{7,3},{8,12},{9,13},{10,... | collective-permute-start | bytes 4718600 | tf_op jit(solution)/shard_map/ppermute | solution.py:10
  388.4 6.8 %copy-start.5 = (f32[256,3072]{1,0:T(8,128)}, f32[256,3072]{1,0:T(8,128)S(1)}, u32[]{:S(2)}) copy-start(f32[256,3072]{1,0:T(8,128)S(1)} %fusion) | copy-start | bytes 9437188
  388.4 7.9 %copy-start.11 = (s32[4,1,1,128]{3,2,1,0:T(1,128)S(1)}, s32[4,1,1,128]{3,2,1,0:T(1,128)}, u32[]{:S(2)}) copy-start(s32[4,1,1,128]{3,2,1,0:T(1,128)} %param.12) | copy-start | bytes 6148
  508.0 2.7 copy-start.1
  508.1 35.3 %collective-permute-start.1 = (f32[128,3072]{1,0:T(8,128)S(1)}, f32[128,3072]{1,0:T(8,128)S(1)}, u32[]{:S(2)}, u32[]{:S(2)}) collective-permute-start(f32[128,3072]{1,0:T(8,128)S(1)} %slice.172), channel_id=1, source_target_pairs={{0,1},{1,0},{2,3},{3,2},{4,5},{5,4},{6,7},{7,6},{8,9},{9,8},{10,11... | collective-permute-start | bytes 4718600 | tf_op jit(solution)/shard_map/ppermute | solution.py:10
  544.5 3.0 copy-start.3
  544.6 2.9 copy-start.9
  554.8 2.7 copy-start.2
  554.9 34.8 %collective-permute-start.2 = (f32[128,3072]{1,0:T(8,128)S(1)}, f32[128,3072]{1,0:T(8,128)S(1)}, u32[]{:S(2)}, u32[]{:S(2)}) collective-permute-start(f32[128,3072]{1,0:T(8,128)S(1)} %slice.177), channel_id=1, source_target_pairs={{0,16},{8,24},{16,0},{24,8},{1,17},{9,25},{17,1},{25,9},{2,18},{10... | collective-permute-start | bytes 4718600 | tf_op jit(solution)/shard_map/ppermute | solution.py:10
  590.9 3.0 copy-start.4
  590.9 2.9 copy-start.8
  601.2 2.7 copy-start
  601.3 5.4 collective-permute-start.3
  607.9 3.0 copy-start.6
  607.9 2.9 copy-start.7
Sparse Core Ops, SparseCore 0:
  13.7 96.7 all-gather.1
  396.4 103.4 all-reduce.3
where the time goes:
time: 639 us; the launch traced here: 627 us
  waiting for transfers between devices  261 us (41%)
  other arithmetic  240 us (38%)
  matrix products  61 us (10%)
  local copies, waits for them, and re-layouts  39.5 us (6%)
  between operations  19.6 us (3%)
    another operation x28, other arithmetic, inverse_factor(): lower_factor = jnp.linalg.cholesky(symmetric)  139 us
    psum x1, waiting for transfers between devices, broadcast(): return lax.psum(block, axis)  99.6 us
    all_gather x1, waiting for transfers between devices, body(): whole_diagonal = lax.all_gather(diagonal_blocks, 'fc', axis=2, tiled=True)  94 us
    another operation x9, other arithmetic, inverse_factor(): lax.linalg.triangular_solve(lower_factor, identity, left_side=True, lower...  79.7 us
    ppermute x4, waiting for transfers between devices, partner(): lax.ppermute(x, axis, [(i, i ^ 1 << distance) for i in range(lax.axis_siz...  67.7 us
    dot_general x4, matrix products, body(): jnp.dot(slab_factor, column_factor.T, precision=HIGHEST)  31.7 us
    dot_general x4, matrix products, body(): column_factor = jnp.dot(panel_level, inverse.T, precision=HIGHEST)  23.9 us
    another operation x29, local copies, waits for them, and re-layouts, inverse_factor(): lax.linalg.triangular_solve(lower_factor, identity, left_side=True, lower...  16.4 us
  transfers between devices with their start and end apart: 6, of which 5 were waited for; matrix products, arithmetic and copies ran while one was open for 46% of the time, Pallas kernels for 0%

commit v1 on v0

v1 whole, which is shorter than its diff:
```python
import functools

import jax
import jax.numpy as jnp
from jax import lax
from jax.experimental import pallas as pl
from jax.experimental.pallas import tpu as pltpu
from jax.sharding import PartitionSpec as P

HIGHEST = lax.Precision.HIGHEST
MESH = pl.DeviceIdType.MESH
F32, BF16 = jnp.float32, jnp.bfloat16
PIVOT = 32
WIDTH = 256
LAG = 5


def split(x):
    high = x.astype(BF16)
    return high, (x - high.astype(F32)).astype(BF16)


def dot_t(a, b):
    return lax.dot_general(a, b, (((1,), (1,)), ((), ())), preferred_element_type=F32)


def product(a_high, a_low, b_high, b_low):
    return dot_t(a_high, b_high) + (dot_t(a_low, b_high) + dot_t(a_high, b_low))


def exact_dot(a, b):
    return jnp.dot(a, b, precision=HIGHEST, preferred_element_type=F32)


def small_inverse(m):
    size = m.shape[0]
    row = lax.broadcasted_iota(jnp.int32, m.shape, 0)
    lane = lax.broadcasted_iota(jnp.int32, m.shape, 1)
    for k in range(size):
        pivot = m[k : k + 1, k : k + 1]
        column = m[:, k : k + 1]
        pivot_row = jnp.where(lane[k : k + 1] == k, 1.0, m[k : k + 1]) / pivot
        m = jnp.where(row == k, pivot_row, jnp.where(lane == k, 0.0, m) - column * pivot_row)
    return m


def pivot_step(work):
    size = work.shape[0]
    w = work[...]
    inverse = small_inverse(w[:PIVOT, :PIVOT])
    lane = lax.broadcasted_iota(jnp.int32, (PIVOT, size), 1)
    sub = lax.broadcasted_iota(jnp.int32, (PIVOT, size), 0)
    top = jnp.where(lane < PIVOT, jnp.where(lane == sub, 1.0, 0.0), w[:PIVOT])
    top = exact_dot(inverse, top)
    below = w[PIVOT:]
    lane = lax.broadcasted_iota(jnp.int32, below.shape, 1)
    below = jnp.where(lane < PIVOT, 0.0, below) - exact_dot(below[:, :PIVOT], top)
    turn = lambda x: jnp.concatenate([x[:, PIVOT:], x[:, :PIVOT]], axis=1)
    work[pl.ds(0, size - PIVOT), :] = turn(below)
    work[pl.ds(size - PIVOT, PIVOT), :] = turn(top)


def kernel(
    n, nr, front_hbm, panels_hbm, diag_hbm, maps_ref, out_hbm,
    front, panels, gathered, work, shared, window, s_high, s_low, moves, received,
    diag_send, diag_recv, window_send, window_recv, window_load, inv_send, inv_recv,
    level_send, level_recv, load_sem, panel_sem, out_sem,
):
    c, r = lax.axis_index("fc"), lax.axis_index("fr")
    levels, pw = panels.shape[0], panels.shape[2]
    rows, cols = front.shape
    block = received.shape[1]
    chunks = cols // WIDTH
    groups = rows // block
    share = pw // n
    half = levels // 2
    even = c % 2 == 0

    barrier = pltpu.get_barrier_semaphore()
    for d in range(1, n):
        pl.semaphore_signal(barrier, inc=1, device_id={"fc": (c + d) % n}, device_id_type=MESH)
    for d in range(1, nr):
        pl.semaphore_signal(barrier, inc=1, device_id={"fr": (r + d) % nr}, device_id_type=MESH)
    own_window = []
    for g in range(groups):
        start = pl.multiple_of((r * rows) % cols + g * block, block)
        own_window.append(pltpu.make_async_copy(
            panels_hbm.at[:, pl.ds(start, block)], window.at[:, pl.ds(g * block, block)], window_load.at[g]
        ))
    front_load = pltpu.make_async_copy(front_hbm, front, load_sem.at[0])
    diag_rows = pl.ds(pl.multiple_of(c * share, 8), share)
    diag_load = pltpu.make_async_copy(diag_hbm, gathered.at[diag_rows], load_sem.at[1])
    diag_load.start()

    @pl.when(c == 0)
    def _():
        for copy in own_window:
            copy.start()

    pl.semaphore_wait(barrier, n - 1 + nr - 1)

    diag_copies = []
    for d in range(1, n):
        diag_copies.append(pltpu.make_async_remote_copy(
            src_ref=diag_hbm, dst_ref=gathered.at[diag_rows],
            send_sem=diag_send.at[d - 1], recv_sem=diag_recv.at[d - 1],
            device_id={"fc": (c + d) % n}, device_id_type=MESH,
        ))
    for copy in diag_copies:
        copy.start()

    def window_copy(g, h, way, target):
        part = window.at[pl.ds(h * half, half), pl.ds(g * block, block)]
        return pltpu.make_async_remote_copy(
            src_ref=part, dst_ref=part,
            send_sem=window_send.at[g, h, way], recv_sem=window_recv.at[g, h],
            device_id={"fc": target % n}, device_id_type=MESH,
        )

    def forwards(g, act):
        @pl.when(even)
        def _():
            act(window_copy(g, 0, 1, c + 1))

            @pl.when(c + 2 < n)
            def _():
                act(window_copy(g, 0, 0, c + 2))

        @pl.when(c == 0)
        def _():
            act(window_copy(g, 1, 0, 1 + c))

        @pl.when(jnp.logical_not(even))
        def _():
            @pl.when(c + 2 < n)
            def _():
                act(window_copy(g, 1, 0, c + 2))

            @pl.when(c >= 3)
            def _():
                act(window_copy(g, 1, 1, c - 1))

    def start(copy):
        copy.start()

    def wait_send(copy):
        copy.wait_send()

    def chain(g):
        @pl.when(c == 0)
        def _():
            own_window[g].wait()

        @pl.when(jnp.logical_and(c > 0, even))
        def _():
            window_copy(g, 0, 0, c + 1).wait_recv()

        @pl.when(jnp.logical_not(even))
        def _():
            window_copy(g, 1, 0, c + 1).wait_recv()

        forwards(g, start)

    def rest_of(g):
        @pl.when(jnp.logical_and(c > 0, even))
        def _():
            window_copy(g, 1, 0, c + 1).wait_recv()

        @pl.when(jnp.logical_not(even))
        def _():
            window_copy(g, 0, 0, c + 1).wait_recv()

    partners = [
        {"fc": (c + n // 2) % n},
        {"fc": c + 1 - 2 * (c % 2)},
        {"fr": (r + nr // 2) % nr},
        {"fr": r + 1 - 2 * (r % 2)},
    ]

    def columns(k):
        return pl.ds(pl.multiple_of(k * WIDTH, WIDTH), WIDTH)

    def level_copy(level, k):
        source = front_hbm if level == 0 else front
        return pltpu.make_async_remote_copy(
            src_ref=source.at[pl.ds(0, block), columns(k)],
            dst_ref=received.at[level, :, columns(k)],
            send_sem=level_send.at[level, k], recv_sem=level_recv.at[level, k],
            device_id=partners[level], device_id_type=MESH,
        )

    def panel_copy(k):
        part = pl.ds(pl.multiple_of(k * WIDTH, WIDTH), WIDTH)
        return pltpu.make_async_copy(panels_hbm.at[:, part], panels.at[:, part], panel_sem.at[k])

    def out_copy(k):
        return pltpu.make_async_copy(front.at[:, columns(k)], out_hbm.at[:, columns(k)], out_sem.at[k])

    @pl.when(c == 0)
    def _():
        chain(0)

    @pl.loop(0, chunks)
    def _(k):
        level_copy(0, k).start()

    @pl.when(c == 0)
    def _():
        for g in range(1, groups):
            chain(g)

    front_load.start()

    @pl.loop(0, chunks)
    def _(k):
        panel_copy(k).start()

    for level in range(levels):
        wanted = maps_ref[pl.ds(level, 1), :]
        index = lax.broadcasted_iota(jnp.int32, (block, block), 0)
        moves[level] = jnp.where(index == wanted, 1.0, 0.0).T.astype(BF16)

    diag_load.wait()
    for copy in diag_copies:
        copy.wait()
    transposed = gathered[...]
    symmetric = 0.5 * (transposed + transposed.T)
    sub = lax.broadcasted_iota(jnp.int32, symmetric.shape, 0)
    lane = lax.broadcasted_iota(jnp.int32, symmetric.shape, 1)
    diagonal = jnp.where(sub == lane, symmetric, 0.0)
    scale_row = lax.rsqrt(jnp.sum(diagonal, axis=0, keepdims=True))
    scale_column = lax.rsqrt(jnp.sum(diagonal, axis=1, keepdims=True))
    work[...] = symmetric * scale_row * scale_column
    shared[r, pl.ds(pw, 8), :] = jnp.broadcast_to(scale_row, (8, pw))

    @pl.loop(0, pw // PIVOT)
    def _(i):
        pivot_step(work)

        @pl.when(jnp.logical_and(c > 0, i == jnp.minimum(c // 2, pw // PIVOT - 1)))
        def _():
            chain(0)

    shared[r, pl.ds(0, pw), :] = work[...]
    inv_copies = []
    for d in range(1, nr):
        inv_copies.append(pltpu.make_async_remote_copy(
            src_ref=shared.at[r], dst_ref=shared.at[r],
            send_sem=inv_send.at[d - 1], recv_sem=inv_recv.at[d - 1],
            device_id={"fr": (r + d) % nr}, device_id_type=MESH,
        ))
    for copy in inv_copies:
        copy.start()
    rest_of(0)
    for copy in inv_copies:
        copy.wait()

    def scaled(x, level):
        return x * shared[level, pl.ds(pw, 1), :]

    def make_s(first, count):
        for level in range(levels):
            part = pl.ds(first, count)
            s = exact_dot(scaled(window[level, part, :], level), shared[level, pl.ds(0, pw), :])
            high, low = split(s)
            s_high[level, part, :] = high
            s_low[level, part, :] = low

    make_s(0, block)
    front_load.wait()

    def update(level, k, part):
        p_high, p_low = split(scaled(panels[level, columns(k), :], level))
        return product(s_high[level, part, :], s_low[level, part, :], p_high, p_low)

    def stage(level, k):
        if level == 0:
            panel_copy(k).wait()
        level_copy(level, k).wait()
        high, low = split(received[level, :, columns(k)])
        move = moves[level]
        moved = jnp.dot(move, high, preferred_element_type=F32) + jnp.dot(move, low, preferred_element_type=F32)
        top = front[pl.ds(0, block), columns(k)] + moved
        front[pl.ds(0, block), columns(k)] = top - update(level, k, pl.ds(0, block))
        if level + 1 < levels:
            level_copy(level + 1, k).start()

    @pl.loop(0, chunks + LAG)
    def _(t):
        for level in reversed(range(levels)):
            @pl.when(jnp.logical_and(t >= level, t < chunks + level))
            def _():
                stage(level, t - level)

        for g in range(1, groups):
            @pl.when(jnp.logical_and(c > 0, t == g - 1))
            def _():
                chain(g)

        @pl.when(t == LAG - 1)
        def _():
            for g in range(1, groups):
                rest_of(g)
                make_s(g * block, block)

        @pl.when(t >= LAG)
        def _():
            k = t - LAG
            part = pl.ds(block, rows - block)
            total = update(0, k, part)
            for level in range(1, levels):
                total = total + update(level, k, part)
            front[part, columns(k)] = front[part, columns(k)] - total
            out_copy(k).start()

    for g in range(groups):
        forwards(g, wait_send)

    @pl.loop(0, chunks)
    def _(k):
        out_copy(k).wait()


def body(front_slab, panels, diagonal_blocks, extend_maps):
    rows, cols = front_slab.shape
    levels, _, pw = panels.shape
    block = extend_maps.shape[3]
    n, nr = lax.axis_size("fc"), lax.axis_size("fr")
    chunks, groups = cols // WIDTH, rows // block
    mine = lax.dynamic_index_in_dim(diagonal_blocks, lax.axis_index("fr"), 0, keepdims=False).T
    anywhere = pl.BlockSpec(memory_space=pl.ANY)
    dma = pltpu.SemaphoreType.DMA
    return pl.pallas_call(
        functools.partial(kernel, n, nr),
        out_shape=jax.ShapeDtypeStruct((rows, cols), F32),
        in_specs=[anywhere, anywhere, anywhere, pl.BlockSpec(memory_space=pltpu.VMEM)],
        out_specs=anywhere,
        scratch_shapes=[
            pltpu.VMEM((rows, cols), F32),
            pltpu.VMEM(panels.shape, F32),
            pltpu.VMEM((pw, pw), F32),
            pltpu.VMEM((pw, pw), F32),
            pltpu.VMEM((levels, pw + 8, pw), F32),
            pltpu.VMEM((levels, rows, pw), F32),
            pltpu.VMEM((levels, rows, pw), BF16),
            pltpu.VMEM((levels, rows, pw), BF16),
            pltpu.VMEM((levels, block, block), BF16),
            pltpu.VMEM((levels, block, cols), F32),
            dma((n - 1,)),
            dma((n - 1,)),
            dma((groups, 2, 2)),
            dma((groups, 2)),
            dma((groups,)),
            dma((nr - 1,)),
            dma((nr - 1,)),
            dma((levels, chunks)),
            dma((levels, chunks)),
            dma((2,)),
            dma((chunks,)),
            dma((chunks,)),
        ],
        compiler_params=pltpu.CompilerParams(
            collective_id=0, has_side_effects=True, vmem_limit_bytes=50 * 2**20
        ),
        cost_estimate=pl.CostEstimate(
            flops=6 * rows * cols * levels * pw, bytes_accessed=8 * rows * cols + 4 * panels.size, transcendentals=0
        ),
    )(front_slab, panels, mine, extend_maps.reshape(levels, block))


def solution(mesh):
    in_specs = (P("fr", "fc"), P(None, "fc", None), P(None, None, "fc"), P(None, "fr", "fc", None))
    return jax.shard_map(body, mesh=mesh, in_specs=in_specs, out_specs=P("fr", "fc"), check_vma=False)
```

time: 639 us -> 203 us (0.32); the launches traced: 627 us -> 203 us
  waiting for transfers between devices: 261 us -> 0 us
  other arithmetic: 240 us -> 0 us
  Pallas kernels: 0 us -> 195 us
  matrix products: 61 us -> 0 us
  local copies, waits for them, and re-layouts: 39.5 us -> 7.82 us
  between operations: 19.6 us -> 0.01 us
    another operation x37 -> x0, other arithmetic: 219 us -> none  [the longest x28 139 us: inverse_factor(): lower_factor = jnp.linalg.cholesky(symmetric)]
    pallas_call x0 -> x1, Pallas kernels: none -> 195 us  [body(): pl.pallas_call(functools.partial(kernel, n, nr), out_shape=jax.ShapeDtype...]
    psum x1 -> x0, waiting for transfers between devices: 99.6 us -> none  [broadcast(): return lax.psum(block, axis)]
    all_gather x1 -> x0, waiting for transfers between devices: 94 us -> none  [body(): whole_diagonal = lax.all_gather(diagonal_blocks, 'fc', axis=2, tiled=True)]
    ppermute x4 -> x0, waiting for transfers between devices: 67.7 us -> none  [partner(): lax.ppermute(x, axis, [(i, i ^ 1 << distance) for i in range(lax.axis_siz...]
    dot_general x8 -> x0, matrix products: 55.6 us -> none  [the longest x4 31.7 us: body(): jnp.dot(slab_factor, column_factor.T, precision=HIGHEST)]
    another operation x37 -> x0, local copies, waits for them, and re-layouts: 16.5 us -> none  [the longest x29 16.4 us: inverse_factor(): lax.linalg.triangular_solve(lower_factor, identity, left_side=True, lower...]
    dynamic_update_slice x4 -> x0, other arithmetic: 11.6 us -> none  [merge_top(): lax.dynamic_update_slice(front_slab, front_slab[:block_rows] + moved_rows...]
  transfers between devices with their start and end apart: 6 -> 0, of which waited for: 5 -> 0; matrix products, arithmetic and copies ran while one was open for 46% -> 0% of each run, Pallas kernels for 0% -> 0%
where the time goes in v1:
time: 203 us
  Pallas kernels  195 us (96%)
  local copies, waits for them, and re-layouts  7.82 us (4%)
    pallas_call x1, Pallas kernels, body(): pl.pallas_call(functools.partial(kernel, n, nr), out_shape=jax.ShapeDtype...  195 us
    unnamed x5, local copies, waits for them, and re-layouts  7.82 us

profile of v1, /device:TPU:25, one launch (start us, length us, event | category | flops | bytes accessed | tf_op | source)
XLA Modules:
  0.0 202.5 jit_solution(1153853790580186646)
XLA Ops:
  0.0 0.0 copy-start
  0.0 0.9 copy-done
  0.9 0.0 copy-start.1
  0.9 0.7 copy-done.1
  1.6 194.7 %shard_map.46 = f32[512,3072]{1,0:T(8,128)} custom-call(f32[512,3072]{1,0:T(8,128)} %front_hbm.1, f32[4,3072,256]{2,1,0:T(8,128)} %panels_hbm.1, f32[32,256]{1,0:T(8,128)S(1)} %dynamic-slice_bitcast_fusion.diag_hbm, s32[4,128]{1,0:T(4,128)S(1)} %bitcast.5), custom_call_target="tpu_custom_call" | custom-call | flops 9663676416 | bytes 25165824 | tf_op jit(solution)/shard_map/pallas_call | solution.py:333
  196.3 6.2 %copy.6 = f32[512,3072]{1,0:T(8,128)} copy(f32[512,3072]{1,0:T(8,128)} %shard_map.46) | data formatting | bytes 12582912
  (1 shorter events, 0.0 us)
Async XLA Ops:
  0.0 0.9 copy-start
  0.9 0.7 copy-start.1

commit v2 on v1

--- a/solution.py
+++ b/solution.py
@@ -12,7 +12,6 @@
 F32, BF16 = jnp.float32, jnp.bfloat16
 PIVOT = 32
 WIDTH = 256
-LAG = 5
 
 
 def split(x):
@@ -22,10 +21,6 @@
 
 def dot_t(a, b):
     return lax.dot_general(a, b, (((1,), (1,)), ((), ())), preferred_element_type=F32)
-
-
-def product(a_high, a_low, b_high, b_low):
-    return dot_t(a_high, b_high) + (dot_t(a_low, b_high) + dot_t(a_high, b_low))
 
 
 def exact_dot(a, b):
@@ -62,7 +57,7 @@
 
 def kernel(
     n, nr, front_hbm, panels_hbm, diag_hbm, maps_ref, out_hbm,
-    front, panels, gathered, work, shared, window, s_high, s_low, moves, received,
+    front, panels, gathered, work, shared, window, factors, moves, received,
     diag_send, diag_recv, window_send, window_recv, window_load, inv_send, inv_recv,
     level_send, level_recv, load_sem, panel_sem, out_sem,
 ):
@@ -117,11 +112,14 @@
             device_id={"fc": target % n}, device_id_type=MESH,
         )
 
+    def across(g, act):
+        @pl.when(even)
+        def _():
+            act(window_copy(g, 0, 1, c + 1))
+
     def forwards(g, act):
         @pl.when(even)
         def _():
-            act(window_copy(g, 0, 1, c + 1))
-
             @pl.when(c + 2 < n)
             def _():
                 act(window_copy(g, 0, 0, c + 2))
@@ -160,6 +158,10 @@
             window_copy(g, 1, 0, c + 1).wait_recv()
 
         forwards(g, start)
+
+        @pl.when(c > 0)
+        def _():
+            across(g, start)
 
     def rest_of(g):
         @pl.when(jnp.logical_and(c > 0, even))
@@ -196,18 +198,22 @@
     def out_copy(k):
         return pltpu.make_async_copy(front.at[:, columns(k)], out_hbm.at[:, columns(k)], out_sem.at[k])
 
+    def start_first_level():
+        @pl.loop(0, chunks)
+        def _(k):
+            level_copy(0, k).start()
+
     @pl.when(c == 0)
     def _():
-        chain(0)
-
-    @pl.loop(0, chunks)
-    def _(k):
-        level_copy(0, k).start()
-
-    @pl.when(c == 0)
+        for g in range(groups):
+            chain(g)
+
+    passes_on = jnp.logical_and(c >= 2, c < n // 2)
+    hop = jnp.minimum(c // 2, pw // PIVOT - groups)
+
+    @pl.when(jnp.logical_not(passes_on))
     def _():
-        for g in range(1, groups):
-            chain(g)
+        start_first_level()
 
     front_load.start()
 
@@ -218,7 +224,8 @@
     for level in range(levels):
         wanted = maps_ref[pl.ds(level, 1), :]
         index = lax.broadcasted_iota(jnp.int32, (block, block), 0)
-        moves[level] = jnp.where(index == wanted, 1.0, 0.0).T.astype(BF16)
+        move = jnp.where(index == wanted, 1.0, 0.0).T.astype(BF16)
+        moves[level] = jnp.concatenate([move, move], axis=1)
 
     diag_load.wait()
     for copy in diag_copies:
@@ -237,9 +244,19 @@
     def _(i):
         pivot_step(work)
 
-        @pl.when(jnp.logical_and(c > 0, i == jnp.minimum(c // 2, pw // PIVOT - 1)))
-        def _():
-            chain(0)
+        for g in range(groups):
+            @pl.when(jnp.logical_and(c > 0, i == hop + g))
+            def _():
+                chain(g)
+
+                if g == groups - 1:
+                    @pl.when(passes_on)
+                    def _():
+                        start_first_level()
+
+            @pl.when(jnp.logical_and(c == 0, i == groups - 1))
+            def _():
+                across(g, start)
 
     shared[r, pl.ds(0, pw), :] = work[...]
     inv_copies = []
@@ -251,70 +268,51 @@
         ))
     for copy in inv_copies:
         copy.start()
-    rest_of(0)
+    for g in range(groups):
+        rest_of(g)
     for copy in inv_copies:
         copy.wait()
 
     def scaled(x, level):
         return x * shared[level, pl.ds(pw, 1), :]
 
-    def make_s(first, count):
-        for level in range(levels):
-            part = pl.ds(first, count)
+    for level in range(levels):
+        for g in range(groups):
+            part = pl.ds(g * block, block)
             s = exact_dot(scaled(window[level, part, :], level), shared[level, pl.ds(0, pw), :])
             high, low = split(s)
-            s_high[level, part, :] = high
-            s_low[level, part, :] = low
-
-    make_s(0, block)
+            factors[level, part, :] = jnp.concatenate([high, low, high], axis=1)
     front_load.wait()
 
-    def update(level, k, part):
-        p_high, p_low = split(scaled(panels[level, columns(k), :], level))
-        return product(s_high[level, part, :], s_low[level, part, :], p_high, p_low)
+    def update(level, k):
+        high, low = split(scaled(panels[level, columns(k), :], level))
+        return dot_t(factors[level], jnp.concatenate([high, high, low], axis=1))
 
     def stage(level, k):
         if level == 0:
             panel_copy(k).wait()
+        total = update(level, k)
+        top, below = pl.ds(0, block), pl.ds(block, rows - block)
         level_copy(level, k).wait()
-        high, low = split(received[level, :, columns(k)])
-        move = moves[level]
-        moved = jnp.dot(move, high, preferred_element_type=F32) + jnp.dot(move, low, preferred_element_type=F32)
-        top = front[pl.ds(0, block), columns(k)] + moved
-        front[pl.ds(0, block), columns(k)] = top - update(level, k, pl.ds(0, block))
+        pair = jnp.concatenate(split(received[level, :, columns(k)]), axis=0)
+        moved = jnp.dot(moves[level], pair, preferred_element_type=F32)
+        front[top, columns(k)] = front[top, columns(k)] + moved - total[:block]
         if level + 1 < levels:
             level_copy(level + 1, k).start()
-
-    @pl.loop(0, chunks + LAG)
+        front[below, columns(k)] = front[below, columns(k)] - total[block:]
+        if level + 1 == levels:
+            out_copy(k).start()
+
+    @pl.loop(0, chunks + levels - 1)
     def _(t):
         for level in reversed(range(levels)):
             @pl.when(jnp.logical_and(t >= level, t < chunks + level))
             def _():
                 stage(level, t - level)
 
-        for g in range(1, groups):
-            @pl.when(jnp.logical_and(c > 0, t == g - 1))
-            def _():
-                chain(g)
-
-        @pl.when(t == LAG - 1)
-        def _():
-            for g in range(1, groups):
-                rest_of(g)
-                make_s(g * block, block)
-
-        @pl.when(t >= LAG)
-        def _():
-            k = t - LAG
-            part = pl.ds(block, rows - block)
-            total = update(0, k, part)
-            for level in range(1, levels):
-                total = total + update(level, k, part)
-            front[part, columns(k)] = front[part, columns(k)] - total
-            out_copy(k).start()
-
     for g in range(groups):
         forwards(g, wait_send)
+        across(g, wait_send)
 
     @pl.loop(0, chunks)
     def _(k):
@@ -342,9 +340,8 @@
             pltpu.VMEM((pw, pw), F32),
             pltpu.VMEM((levels, pw + 8, pw), F32),
             pltpu.VMEM((levels, rows, pw), F32),
-            pltpu.VMEM((levels, rows, pw), BF16),
-            pltpu.VMEM((levels, rows, pw), BF16),
-            pltpu.VMEM((levels, block, block), BF16),
+            pltpu.VMEM((levels, rows, 3 * pw), BF16),
+            pltpu.VMEM((levels, block, 2 * block), BF16),
             pltpu.VMEM((levels, block, cols), F32),
             dma((n - 1,)),
             dma((n - 1,)),

time: 203 us -> 222 us (1.094)
  Pallas kernels: 195 us -> 213 us
    pallas_call x1, Pallas kernels: 195 us -> 213 us  [body(): pl.pallas_call(functools.partial(kernel, n, nr), out_shape=jax.ShapeDtype...]
where the time goes in v2:
time: 222 us; the launch traced here: 220 us
  Pallas kernels  213 us (96%)
  local copies, waits for them, and re-layouts  7.82 us (4%)
    pallas_call x1, Pallas kernels, body(): pl.pallas_call(functools.partial(kernel, n, nr), out_shape=jax.ShapeDtype...  213 us
    unnamed x5, local copies, waits for them, and re-layouts  7.82 us

profile of v2, /device:TPU:25, one launch (start us, length us, event | category | flops | bytes accessed | tf_op | source)
XLA Modules:
  0.0 220.5 jit_solution(9289495284415277262)
XLA Ops:
  0.0 0.0 copy-start
  0.0 0.9 copy-done
  0.9 0.0 copy-start.1
  0.9 0.7 copy-done.1
  1.6 212.7 %shard_map.46 = f32[512,3072]{1,0:T(8,128)} custom-call(f32[512,3072]{1,0:T(8,128)} %front_hbm.1, f32[4,3072,256]{2,1,0:T(8,128)} %panels_hbm.1, f32[32,256]{1,0:T(8,128)S(1)} %dynamic-slice_bitcast_fusion.diag_hbm, s32[4,128]{1,0:T(4,128)S(1)} %bitcast.5), custom_call_target="tpu_custom_call" | custom-call | flops 9663676416 | bytes 25165824 | tf_op jit(solution)/shard_map/pallas_call | solution.py:331
  214.3 6.2 %copy.6 = f32[512,3072]{1,0:T(8,128)} copy(f32[512,3072]{1,0:T(8,128)} %shard_map.46) | data formatting | bytes 12582912
  (1 shorter events, 0.0 us)
Async XLA Ops:
  0.0 0.9 copy-start
  0.9 0.7 copy-start.1

commit v3 on v2

--- a/solution.py
+++ b/solution.py
@@ -28,15 +28,39 @@
 
 
 def small_inverse(m):
-    size = m.shape[0]
-    row = lax.broadcasted_iota(jnp.int32, m.shape, 0)
-    lane = lax.broadcasted_iota(jnp.int32, m.shape, 1)
-    for k in range(size):
-        pivot = m[k : k + 1, k : k + 1]
-        column = m[:, k : k + 1]
-        pivot_row = jnp.where(lane[k : k + 1] == k, 1.0, m[k : k + 1]) / pivot
-        m = jnp.where(row == k, pivot_row, jnp.where(lane == k, 0.0, m) - column * pivot_row)
-    return m
+    size, group = m.shape[0], 8
+    shape = (group, size)
+    sub = lax.broadcasted_iota(jnp.int32, shape, 0)
+    lane = lax.broadcasted_iota(jnp.int32, shape, 1)
+    parts = [m[i : i + group] for i in range(0, size, group)]
+
+    def row_of(x, k):
+        return jnp.broadcast_to(x[k : k + 1], shape)
+
+    for q in range(size // group):
+        spread = [
+            [jnp.broadcast_to(part[:, q * group + j : q * group + j + 1], shape) for j in range(group)]
+            for part in parts
+        ]
+        rows, columns = parts[q], list(spread[q])
+        for k in range(group):
+            at = q * group + k
+            column = columns[k]
+            scale = 1.0 / row_of(column, k)
+            pivot_row = jnp.where(lane == at, scale, row_of(rows, k) * scale)
+            rows = jnp.where(sub == k, pivot_row, jnp.where(lane == at, 0.0, rows) - column * pivot_row)
+            for j in range(k + 1, group):
+                other = row_of(columns[j], k) * scale
+                columns[j] = jnp.where(sub == k, other, columns[j] - column * other)
+        inside = jnp.logical_and(lane >= q * group, lane < (q + 1) * group)
+        for i in range(len(parts)):
+            if i != q:
+                part = jnp.where(inside, 0.0, parts[i])
+                for j in range(group):
+                    part = part - spread[i][j] * row_of(rows, j)
+                parts[i] = part
+        parts[q] = rows
+    return jnp.concatenate(parts, axis=0)
 
 
 def pivot_step(work):

time: 222 us -> 220 us (level)
  no operation moved by 1% of the time
where the time goes in v3:
time: 220 us; the launch traced here: 219 us
  Pallas kernels  211 us (96%)
  local copies, waits for them, and re-layouts  7.82 us (4%)
    pallas_call x1, Pallas kernels, body(): pl.pallas_call(functools.partial(kernel, n, nr), out_shape=jax.ShapeDtype...  211 us
    unnamed x5, local copies, waits for them, and re-layouts  7.82 us

profile of v3, /device:TPU:25, one launch (start us, length us, event | category | flops | bytes accessed | tf_op | source)
XLA Modules:
  0.0 218.8 jit_solution(11971843274548883659)
XLA Ops:
  0.0 0.0 copy-start
  0.0 0.9 copy-done
  0.9 0.0 copy-start.1
  0.9 0.7 copy-done.1
  1.6 210.9 %shard_map.46 = f32[512,3072]{1,0:T(8,128)} custom-call(f32[512,3072]{1,0:T(8,128)} %front_hbm.1, f32[4,3072,256]{2,1,0:T(8,128)} %panels_hbm.1, f32[32,256]{1,0:T(8,128)S(1)} %dynamic-slice_bitcast_fusion.diag_hbm, s32[4,128]{1,0:T(4,128)S(1)} %bitcast.5), custom_call_target="tpu_custom_call" | custom-call | flops 9663676416 | bytes 25165824 | tf_op jit(solution)/shard_map/pallas_call | solution.py:355
  212.5 6.2 %copy.6 = f32[512,3072]{1,0:T(8,128)} copy(f32[512,3072]{1,0:T(8,128)} %shard_map.46) | data formatting | bytes 12582912
  (1 shorter events, 0.0 us)
Async XLA Ops:
  0.0 0.9 copy-start
  0.9 0.7 copy-start.1

commit v4 on v3

--- a/solution.py
+++ b/solution.py
@@ -12,6 +12,8 @@
 F32, BF16 = jnp.float32, jnp.bfloat16
 PIVOT = 32
 WIDTH = 256
+SKEW = 2
+EARLY = 2
 
 
 def split(x):
@@ -222,8 +224,8 @@
     def out_copy(k):
         return pltpu.make_async_copy(front.at[:, columns(k)], out_hbm.at[:, columns(k)], out_sem.at[k])
 
-    def start_first_level():
-        @pl.loop(0, chunks)
+    def start_first_level(first, end):
+        @pl.loop(first, end)
         def _(k):
             level_copy(0, k).start()
 
@@ -232,12 +234,16 @@
         for g in range(groups):
             chain(g)
 
-    passes_on = jnp.logical_and(c >= 2, c < n // 2)
-    hop = jnp.minimum(c // 2, pw // PIVOT - groups)
-
-    @pl.when(jnp.logical_not(passes_on))
+    upper = c >= n // 2
+    hop = jnp.minimum(c // 2 - 1, pw // PIVOT - groups)
+
+    @pl.when(c >= 2)
     def _():
-        start_first_level()
+        start_first_level(0, EARLY)
+
+    @pl.when(upper)
+    def _():
+        start_first_level(EARLY, chunks)
 
     front_load.start()
 
@@ -269,43 +275,57 @@
         pivot_step(work)
 
         for g in range(groups):
-            @pl.when(jnp.logical_and(c > 0, i == hop + g))
+            @pl.when(jnp.logical_and(c > 0, i == jnp.maximum(hop + g, 0)))
             def _():
                 chain(g)
 
-                if g == groups - 1:
-                    @pl.when(passes_on)
-                    def _():
-                        start_first_level()
-
             @pl.when(jnp.logical_and(c == 0, i == groups - 1))
             def _():
                 across(g, start)
 
+        @pl.when(jnp.logical_and(c < 2, i == groups - 1))
+        def _():
+            start_first_level(0, EARLY)
+
+        @pl.when(jnp.logical_and(jnp.logical_not(upper), i == jnp.maximum(hop, 0) + groups - 1))
+        def _():
+            start_first_level(EARLY, chunks)
+
     shared[r, pl.ds(0, pw), :] = work[...]
-    inv_copies = []
-    for d in range(1, nr):
-        inv_copies.append(pltpu.make_async_remote_copy(
-            src_ref=shared.at[r], dst_ref=shared.at[r],
-            send_sem=inv_send.at[d - 1], recv_sem=inv_recv.at[d - 1],
-            device_id={"fr": (r + d) % nr}, device_id_type=MESH,
-        ))
-    for copy in inv_copies:
-        copy.start()
+    def inv_copy(index, slot, target):
+        return pltpu.make_async_remote_copy(
+            src_ref=shared.at[slot], dst_ref=shared.at[slot],
+            send_sem=inv_send.at[index], recv_sem=inv_recv.at[index],
+            device_id=target, device_id_type=MESH,
+        )
+
+    far, near = partners[2], partners[3]
+    far_copy = inv_copy(0, r, far)
+    near_copy = inv_copy(1, r, near)
+    pass_copy = inv_copy(2, far["fr"], near)
+    far_copy.start()
+    near_copy.start()
+    far_copy.wait_recv()
+    pass_copy.start()
     for g in range(groups):
         rest_of(g)
-    for copy in inv_copies:
-        copy.wait()
+    far_copy.wait_send()
+    near_copy.wait()
+    pass_copy.wait()
 
     def scaled(x, level):
         return x * shared[level, pl.ds(pw, 1), :]
 
     for level in range(levels):
-        for g in range(groups):
-            part = pl.ds(g * block, block)
-            s = exact_dot(scaled(window[level, part, :], level), shared[level, pl.ds(0, pw), :])
-            high, low = split(s)
-            factors[level, part, :] = jnp.concatenate([high, low, high], axis=1)
+        x_high, x_low = split(scaled(window[level], level))
+        high, low = split(shared[level, pl.ds(0, pw), :])
+        s = jnp.dot(
+            jnp.concatenate([x_high, x_low, x_high], axis=1),
+            jnp.concatenate([high, high, low], axis=0),
+            preferred_element_type=F32,
+        )
+        high, low = split(s)
+        factors[level] = jnp.concatenate([high, low, high], axis=1)
     front_load.wait()
 
     def update(level, k):
@@ -327,12 +347,12 @@
         if level + 1 == levels:
             out_copy(k).start()
 
-    @pl.loop(0, chunks + levels - 1)
+    @pl.loop(0, chunks + SKEW * (levels - 1))
     def _(t):
         for level in reversed(range(levels)):
-            @pl.when(jnp.logical_and(t >= level, t < chunks + level))
-            def _():
-                stage(level, t - level)
+            @pl.when(jnp.logical_and(t >= SKEW * level, t < chunks + SKEW * level))
+            def _():
+                stage(level, t - SKEW * level)
 
     for g in range(groups):
         forwards(g, wait_send)

time: 220 us -> 191 us (0.87)
  Pallas kernels: 211 us -> 183 us
    pallas_call x1, Pallas kernels: 211 us -> 183 us  [body(): pl.pallas_call(functools.partial(kernel, n, nr), out_shape=jax.ShapeDtype...]
where the time goes in v4:
time: 191 us
  Pallas kernels  183 us (96%)
  local copies, waits for them, and re-layouts  7.82 us (4%)
    pallas_call x1, Pallas kernels, body(): pl.pallas_call(functools.partial(kernel, n, nr), out_shape=jax.ShapeDtype...  183 us
    unnamed x5, local copies, waits for them, and re-layouts  7.82 us

profile of v4, /device:TPU:25, one launch (start us, length us, event | category | flops | bytes accessed | tf_op | source)
XLA Modules:
  0.0 191.2 jit_solution(10379679305454305719)
XLA Ops:
  0.0 0.0 copy-start
  0.0 0.9 copy-done
  0.9 0.0 copy-start.1
  0.9 0.7 copy-done.1
  1.6 183.4 %shard_map.46 = f32[512,3072]{1,0:T(8,128)} custom-call(f32[512,3072]{1,0:T(8,128)} %front_hbm.1, f32[4,3072,256]{2,1,0:T(8,128)} %panels_hbm.1, f32[32,256]{1,0:T(8,128)S(1)} %dynamic-slice_bitcast_fusion.diag_hbm, s32[4,128]{1,0:T(4,128)S(1)} %bitcast.5), custom_call_target="tpu_custom_call" | custom-call | flops 9663676416 | bytes 25165824 | tf_op jit(solution)/shard_map/pallas_call | solution.py:375
  185.0 6.2 %copy.6 = f32[512,3072]{1,0:T(8,128)} copy(f32[512,3072]{1,0:T(8,128)} %shard_map.46) | data formatting | bytes 12582912
  (1 shorter events, 0.0 us)
Async XLA Ops:
  0.0 0.9 copy-start
  0.9 0.7 copy-start.1

commit v5 on v4

--- a/solution.py
+++ b/solution.py
@@ -235,7 +235,11 @@
             chain(g)
 
     upper = c >= n // 2
-    hop = jnp.minimum(c // 2 - 1, pw // PIVOT - groups)
+    steps = pw // PIVOT
+    hops = c // 2 + c % 2
+
+    def relay_step(g):
+        return 2 * (g + hops) - 1
 
     @pl.when(c >= 2)
     def _():
@@ -270,26 +274,14 @@
     work[...] = symmetric * scale_row * scale_column
     shared[r, pl.ds(pw, 8), :] = jnp.broadcast_to(scale_row, (8, pw))
 
-    @pl.loop(0, pw // PIVOT)
+    @pl.loop(0, steps)
     def _(i):
         pivot_step(work)
 
         for g in range(groups):
-            @pl.when(jnp.logical_and(c > 0, i == jnp.maximum(hop + g, 0)))
+            @pl.when(jnp.logical_and(c > 0, i == relay_step(g)))
             def _():
                 chain(g)
-
-            @pl.when(jnp.logical_and(c == 0, i == groups - 1))
-            def _():
-                across(g, start)
-
-        @pl.when(jnp.logical_and(c < 2, i == groups - 1))
-        def _():
-            start_first_level(0, EARLY)
-
-        @pl.when(jnp.logical_and(jnp.logical_not(upper), i == jnp.maximum(hop, 0) + groups - 1))
-        def _():
-            start_first_level(EARLY, chunks)
 
     shared[r, pl.ds(0, pw), :] = work[...]
     def inv_copy(index, slot, target):
@@ -305,6 +297,24 @@
     pass_copy = inv_copy(2, far["fr"], near)
     far_copy.start()
     near_copy.start()
+    for g in range(groups):
+        @pl.when(jnp.logical_and(c > 0, relay_step(g) >= steps))
+        def _():
+            chain(g)
+
+        @pl.when(c == 0)
+        def _():
+            forwards(g, wait_send)
+            across(g, start)
+
+    @pl.when(jnp.logical_not(upper))
+    def _():
+        @pl.when(c < 2)
+        def _():
+            start_first_level(0, EARLY)
+
+        start_first_level(EARLY, chunks)
+
     far_copy.wait_recv()
     pass_copy.start()
     for g in range(groups):
@@ -355,7 +365,10 @@
                 stage(level, t - SKEW * level)
 
     for g in range(groups):
-        forwards(g, wait_send)
+        @pl.when(c > 0)
+        def _():
+            forwards(g, wait_send)
+
         across(g, wait_send)
 
     @pl.loop(0, chunks)

time: 191 us -> 188 us (0.984)
  Pallas kernels: 183 us -> 180 us
    pallas_call x1, Pallas kernels: 183 us -> 180 us  [body(): pl.pallas_call(functools.partial(kernel, n, nr), out_shape=jax.ShapeDtype...]
where the time goes in v5:
time: 188 us
  Pallas kernels  180 us (96%)
  local copies, waits for them, and re-layouts  7.82 us (4%)
    pallas_call x1, Pallas kernels, body(): pl.pallas_call(functools.partial(kernel, n, nr), out_shape=jax.ShapeDtype...  180 us
    unnamed x5, local copies, waits for them, and re-layouts  7.82 us

profile of v5, /device:TPU:25, one launch (start us, length us, event | category | flops | bytes accessed | tf_op | source)
XLA Modules:
  0.0 188.3 jit_solution(6542894568827748236)
XLA Ops:
  0.0 0.0 copy-start
  0.0 0.9 copy-done
  0.9 0.0 copy-start.1
  0.9 0.7 copy-done.1
  1.6 180.5 %shard_map.46 = f32[512,3072]{1,0:T(8,128)} custom-call(f32[512,3072]{1,0:T(8,128)} %front_hbm.1, f32[4,3072,256]{2,1,0:T(8,128)} %panels_hbm.1, f32[32,256]{1,0:T(8,128)S(1)} %dynamic-slice_bitcast_fusion.diag_hbm, s32[4,128]{1,0:T(4,128)S(1)} %bitcast.5), custom_call_target="tpu_custom_call" | custom-call | flops 9663676416 | bytes 25165824 | tf_op jit(solution)/shard_map/pallas_call | solution.py:388
  182.1 6.2 %copy.6 = f32[512,3072]{1,0:T(8,128)} copy(f32[512,3072]{1,0:T(8,128)} %shard_map.46) | data formatting | bytes 12582912
  (1 shorter events, 0.0 us)
Async XLA Ops:
  0.0 0.9 copy-start
  0.9 0.7 copy-start.1

commit v6 on v5

--- a/solution.py
+++ b/solution.py
@@ -13,7 +13,6 @@
 PIVOT = 32
 WIDTH = 256
 SKEW = 2
-EARLY = 2
 
 
 def split(x):
@@ -85,13 +84,13 @@
     n, nr, front_hbm, panels_hbm, diag_hbm, maps_ref, out_hbm,
     front, panels, gathered, work, shared, window, factors, moves, received,
     diag_send, diag_recv, window_send, window_recv, window_load, inv_send, inv_recv,
-    level_send, level_recv, load_sem, panel_sem, out_sem,
+    level_send, level_recv, load_sem, front_sem, panel_sem, out_sem,
 ):
     c, r = lax.axis_index("fc"), lax.axis_index("fr")
     levels, pw = panels.shape[0], panels.shape[2]
-    rows, cols = front.shape
-    block = received.shape[1]
-    chunks = cols // WIDTH
+    chunks, rows, _ = front.shape
+    cols = chunks * WIDTH
+    block = received.shape[2]
     groups = rows // block
     share = pw // n
     half = levels // 2
@@ -108,15 +107,24 @@
         own_window.append(pltpu.make_async_copy(
             panels_hbm.at[:, pl.ds(start, block)], window.at[:, pl.ds(g * block, block)], window_load.at[g]
         ))
-    front_load = pltpu.make_async_copy(front_hbm, front, load_sem.at[0])
     diag_rows = pl.ds(pl.multiple_of(c * share, 8), share)
-    diag_load = pltpu.make_async_copy(diag_hbm, gathered.at[diag_rows], load_sem.at[1])
+    diag_load = pltpu.make_async_copy(diag_hbm, gathered.at[diag_rows], load_sem)
     diag_load.start()
 
     @pl.when(c == 0)
     def _():
         for copy in own_window:
             copy.start()
+
+    def columns(k):
+        return pl.ds(pl.multiple_of(k * WIDTH, WIDTH), WIDTH)
+
+    def front_copy(k):
+        return pltpu.make_async_copy(front_hbm.at[:, columns(k)], front.at[k], front_sem.at[k])
+
+    @pl.loop(0, chunks)
+    def _(k):
+        front_copy(k).start()
 
     pl.semaphore_wait(barrier, n - 1 + nr - 1)
 
@@ -205,14 +213,10 @@
         {"fr": r + 1 - 2 * (r % 2)},
     ]
 
-    def columns(k):
-        return pl.ds(pl.multiple_of(k * WIDTH, WIDTH), WIDTH)
-
     def level_copy(level, k):
-        source = front_hbm if level == 0 else front
         return pltpu.make_async_remote_copy(
-            src_ref=source.at[pl.ds(0, block), columns(k)],
-            dst_ref=received.at[level, :, columns(k)],
+            src_ref=front.at[k, pl.ds(0, block)],
+            dst_ref=received.at[level, k],
             send_sem=level_send.at[level, k], recv_sem=level_recv.at[level, k],
             device_id=partners[level], device_id_type=MESH,
         )
@@ -222,7 +226,7 @@
         return pltpu.make_async_copy(panels_hbm.at[:, part], panels.at[:, part], panel_sem.at[k])
 
     def out_copy(k):
-        return pltpu.make_async_copy(front.at[:, columns(k)], out_hbm.at[:, columns(k)], out_sem.at[k])
+        return pltpu.make_async_copy(front.at[k], out_hbm.at[:, columns(k)], out_sem.at[k])
 
     def start_first_level(first, end):
         @pl.loop(first, end)
@@ -234,22 +238,22 @@
         for g in range(groups):
             chain(g)
 
+    @pl.loop(0, chunks)
+    def _(k):
+        front_copy(k).wait()
+
     upper = c >= n // 2
     steps = pw // PIVOT
     hops = c // 2 + c % 2
 
     def relay_step(g):
-        return 2 * (g + hops) - 1
-
-    @pl.when(c >= 2)
-    def _():
-        start_first_level(0, EARLY)
+        return g + hops
+
+    lower_relay = jnp.logical_and(c > 0, jnp.logical_not(upper))
 
     @pl.when(upper)
     def _():
-        start_first_level(EARLY, chunks)
-
-    front_load.start()
+        start_first_level(0, chunks)
 
     @pl.loop(0, chunks)
     def _(k):
@@ -283,6 +287,14 @@
             def _():
                 chain(g)
 
+            @pl.when(jnp.logical_and(c == 0, i == steps - groups + g))
+            def _():
+                across(g, start)
+
+        @pl.when(jnp.logical_and(lower_relay, i == relay_step(groups - 1)))
+        def _():
+            start_first_level(0, chunks)
+
     shared[r, pl.ds(0, pw), :] = work[...]
     def inv_copy(index, slot, target):
         return pltpu.make_async_remote_copy(
@@ -305,15 +317,10 @@
         @pl.when(c == 0)
         def _():
             forwards(g, wait_send)
-            across(g, start)
-
-    @pl.when(jnp.logical_not(upper))
+
+    @pl.when(jnp.logical_or(c == 0, jnp.logical_and(lower_relay, relay_step(groups - 1) >= steps)))
     def _():
-        @pl.when(c < 2)
-        def _():
-            start_first_level(0, EARLY)
-
-        start_first_level(EARLY, chunks)
+        start_first_level(0, chunks)
 
     far_copy.wait_recv()
     pass_copy.start()
@@ -336,8 +343,6 @@
         )
         high, low = split(s)
         factors[level] = jnp.concatenate([high, low, high], axis=1)
-    front_load.wait()
-
     def update(level, k):
         high, low = split(scaled(panels[level, columns(k), :], level))
         return dot_t(factors[level], jnp.concatenate([high, high, low], axis=1))
@@ -348,12 +353,12 @@
         total = update(level, k)
         top, below = pl.ds(0, block), pl.ds(block, rows - block)
         level_copy(level, k).wait()
-        pair = jnp.concatenate(split(received[level, :, columns(k)]), axis=0)
+        pair = jnp.concatenate(split(received[level, k]), axis=0)
         moved = jnp.dot(moves[level], pair, preferred_element_type=F32)
-        front[top, columns(k)] = front[top, columns(k)] + moved - total[:block]
+        front[k, top, :] = front[k, top, :] + moved - total[:block]
         if level + 1 < levels:
             level_copy(level + 1, k).start()
-        front[below, columns(k)] = front[below, columns(k)] - total[block:]
+        front[k, below, :] = front[k, below, :] - total[block:]
         if level + 1 == levels:
             out_copy(k).start()
 
@@ -391,7 +396,7 @@
         in_specs=[anywhere, anywhere, anywhere, pl.BlockSpec(memory_space=pltpu.VMEM)],
         out_specs=anywhere,
         scratch_shapes=[
-            pltpu.VMEM((rows, cols), F32),
+            pltpu.VMEM((chunks, rows, WIDTH), F32),
             pltpu.VMEM(panels.shape, F32),
             pltpu.VMEM((pw, pw), F32),
             pltpu.VMEM((pw, pw), F32),
@@ -399,7 +404,7 @@
             pltpu.VMEM((levels, rows, pw), F32),
             pltpu.VMEM((levels, rows, 3 * pw), BF16),
             pltpu.VMEM((levels, block, 2 * block), BF16),
-            pltpu.VMEM((levels, block, cols), F32),
+            pltpu.VMEM((levels, chunks, block, WIDTH), F32),
             dma((n - 1,)),
             dma((n - 1,)),
             dma((groups, 2, 2)),
@@ -409,7 +414,8 @@
             dma((nr - 1,)),
             dma((levels, chunks)),
             dma((levels, chunks)),
-            dma((2,)),
+            dma,
+            dma((chunks,)),
             dma((chunks,)),
             dma((chunks,)),
         ],

time: 188 us -> 194 us (1.032)
  Pallas kernels: 180 us -> 186 us
    pallas_call x1, Pallas kernels: 180 us -> 186 us  [body(): pl.pallas_call(functools.partial(kernel, n, nr), out_shape=jax.ShapeDtype...]
where the time goes in v6:
time: 194 us
  Pallas kernels  186 us (96%)
  local copies, waits for them, and re-layouts  7.82 us (4%)
    pallas_call x1, Pallas kernels, body(): pl.pallas_call(functools.partial(kernel, n, nr), out_shape=jax.ShapeDtype...  186 us
    unnamed x5, local copies, waits for them, and re-layouts  7.82 us

profile of v6, /device:TPU:25, one launch (start us, length us, event | category | flops | bytes accessed | tf_op | source)
XLA Modules:
  0.0 193.6 jit_solution(2746171188966320138)
XLA Ops:
  0.0 0.0 copy-start
  0.0 0.9 copy-done
  0.9 0.0 copy-start.1
  0.9 0.7 copy-done.1
  1.6 185.8 %shard_map.46 = f32[512,3072]{1,0:T(8,128)} custom-call(f32[512,3072]{1,0:T(8,128)} %front_hbm.1, f32[4,3072,256]{2,1,0:T(8,128)} %panels_hbm.1, f32[32,256]{1,0:T(8,128)S(1)} %dynamic-slice_bitcast_fusion.diag_hbm, s32[4,128]{1,0:T(4,128)S(1)} %bitcast.5), custom_call_target="tpu_custom_call" | custom-call | flops 9663676416 | bytes 25165824 | tf_op jit(solution)/shard_map/pallas_call | solution.py:393
  187.4 6.2 %copy.6 = f32[512,3072]{1,0:T(8,128)} copy(f32[512,3072]{1,0:T(8,128)} %shard_map.46) | data formatting | bytes 12582912
  (1 shorter events, 0.0 us)
Async XLA Ops:
  0.0 0.9 copy-start
  0.9 0.7 copy-start.1

commit v7 on v6

--- a/solution.py
+++ b/solution.py
@@ -13,6 +13,7 @@
 PIVOT = 32
 WIDTH = 256
 SKEW = 2
+OPEN = 4
 
 
 def split(x):
@@ -235,8 +236,7 @@
 
     @pl.when(c == 0)
     def _():
-        for g in range(groups):
-            chain(g)
+        chain(0)
 
     @pl.loop(0, chunks)
     def _(k):
@@ -249,11 +249,9 @@
     def relay_step(g):
         return g + hops
 
-    lower_relay = jnp.logical_and(c > 0, jnp.logical_not(upper))
-
     @pl.when(upper)
     def _():
-        start_first_level(0, chunks)
+        start_first_level(0, OPEN)
 
     @pl.loop(0, chunks)
     def _(k):
@@ -291,9 +289,24 @@
             def _():
                 across(g, start)
 
-        @pl.when(jnp.logical_and(lower_relay, i == relay_step(groups - 1)))
-        def _():
-            start_first_level(0, chunks)
+            if g:
+                @pl.when(jnp.logical_and(c == 0, i == g - 1))
+                def _():
+                    forwards(g - 1, wait_send)
+                    chain(g)
+
+        @pl.when(jnp.logical_and(upper, i % 2 == 1))
+        def _():
+            level_copy(0, i // 2).wait_send()
+            level_copy(0, i // 2 + OPEN).start()
+
+        @pl.when(jnp.logical_and(jnp.logical_not(upper), i == steps // 2))
+        def _():
+            start_first_level(0, OPEN)
+
+        @pl.when(jnp.logical_and(jnp.logical_not(upper), i == steps - 1))
+        def _():
+            start_first_level(OPEN, 2 * OPEN)
 
     shared[r, pl.ds(0, pw), :] = work[...]
     def inv_copy(index, slot, target):
@@ -314,13 +327,9 @@
         def _():
             chain(g)
 
-        @pl.when(c == 0)
-        def _():
-            forwards(g, wait_send)
-
-    @pl.when(jnp.logical_or(c == 0, jnp.logical_and(lower_relay, relay_step(groups - 1) >= steps)))
+    @pl.when(c == 0)
     def _():
-        start_first_level(0, chunks)
+        forwards(groups - 1, wait_send)
 
     far_copy.wait_recv()
     pass_copy.start()
@@ -347,27 +356,55 @@
         high, low = split(scaled(panels[level, columns(k), :], level))
         return dot_t(factors[level], jnp.concatenate([high, high, low], axis=1))
 
-    def stage(level, k):
+    @pl.when(jnp.logical_not(upper))
+    def _():
+        @pl.loop(0, OPEN)
+        def _(k):
+            level_copy(0, k).wait_send()
+
+    def arrive(level, k):
         if level == 0:
             panel_copy(k).wait()
+            level_copy(level, k).wait_recv()
+
+            @pl.when(k >= 2 * OPEN)
+            def _():
+                level_copy(level, k).wait_send()
+
+            @pl.when(k + 2 * OPEN < chunks)
+            def _():
+                level_copy(level, k + OPEN).wait_send()
+                level_copy(level, k + 2 * OPEN).start()
+
+            @pl.when(jnp.logical_and(k + 2 * OPEN >= chunks, k < OPEN))
+            def _():
+                level_copy(level, k + OPEN).wait_send()
+        else:
+            level_copy(level, k).wait()
+
+    def stage(level, k):
         total = update(level, k)
         top, below = pl.ds(0, block), pl.ds(block, rows - block)
-        level_copy(level, k).wait()
         pair = jnp.concatenate(split(received[level, k]), axis=0)
         moved = jnp.dot(moves[level], pair, preferred_element_type=F32)
         front[k, top, :] = front[k, top, :] + moved - total[:block]
+        front[k, below, :] = front[k, below, :] - total[block:]
+
+    def leave(level, k):
         if level + 1 < levels:
             level_copy(level + 1, k).start()
-        front[k, below, :] = front[k, below, :] - total[block:]
-        if level + 1 == levels:
+        else:
             out_copy(k).start()
 
-    @pl.loop(0, chunks + SKEW * (levels - 1))
-    def _(t):
-        for level in reversed(range(levels)):
-            @pl.when(jnp.logical_and(t >= SKEW * level, t < chunks + SKEW * level))
-            def _():
-                stage(level, t - SKEW * level)
+    marks = sorted({SKEW * level + end for level in range(levels) for end in (0, chunks)})
+    for first, end in zip(marks, marks[1:]):
+        active = [x for x in reversed(range(levels)) if SKEW * x <= first < chunks + SKEW * x]
+
+        @pl.loop(first, end)
+        def _(t, active=active):
+            for act in (arrive, stage, leave):
+                for level in active:
+                    act(level, t - SKEW * level)
 
     for g in range(groups):
         @pl.when(c > 0)

time: 194 us -> 192 us (0.990)
  Pallas kernels: 186 us -> 184 us
where the time goes in v7:
time: 192 us
  Pallas kernels  184 us (96%)
  local copies, waits for them, and re-layouts  7.82 us (4%)
    pallas_call x1, Pallas kernels, body(): pl.pallas_call(functools.partial(kernel, n, nr), out_shape=jax.ShapeDtype...  184 us
    unnamed x5, local copies, waits for them, and re-layouts  7.82 us

profile of v7, /device:TPU:25, one launch (start us, length us, event | category | flops | bytes accessed | tf_op | source)
XLA Modules:
  0.0 191.8 jit_solution(17726777129593294195)
XLA Ops:
  0.0 0.0 copy-start
  0.0 0.9 copy-done
  0.9 0.0 copy-start.1
  0.9 0.7 copy-done.1
  1.6 184.0 %shard_map.46 = f32[512,3072]{1,0:T(8,128)} custom-call(f32[512,3072]{1,0:T(8,128)} %front_hbm.1, f32[4,3072,256]{2,1,0:T(8,128)} %panels_hbm.1, f32[32,256]{1,0:T(8,128)S(1)} %dynamic-slice_bitcast_fusion.diag_hbm, s32[4,128]{1,0:T(4,128)S(1)} %bitcast.5), custom_call_target="tpu_custom_call" | custom-call | flops 9663676416 | bytes 25165824 | tf_op jit(solution)/shard_map/pallas_call | solution.py:430
  185.6 6.2 %copy.6 = f32[512,3072]{1,0:T(8,128)} copy(f32[512,3072]{1,0:T(8,128)} %shard_map.46) | data formatting | bytes 12582912
  (1 shorter events, 0.0 us)
Async XLA Ops:
  0.0 0.9 copy-start
  0.9 0.7 copy-start.1
